TPU v7x, 32 devices: a whole 2x2x4 slice. The times are simulated.
32 devices in a mesh: dp: 2 (over x), expert: 8 (over z, core), tensor: 2 (over y).
Axes of the slice: x: 2, y: 2, z: 4, core: 2. Of those that a mesh axis runs over, the one named last changes fastest.
Arguments:
- tokens: bfloat16 [256, 2048], P(('dp', 'expert')), may hold values from -6 to 6
- routes: int32 [256, 8], P(('dp', 'expert')), may hold values from 0 to 15, all different within a row; in each aligned block of 16 rows (0 to 15, 16 to 31, ...) at most 16 rows name the same one
- route_weight: float32 [256, 8], P(('dp', 'expert')), may hold values from 0.02 to 0.5
- weights_gate_up: bfloat16 [16, 2048, 2, 768], P('expert', None, None, 'tensor'), may hold values from -0.125 to 0.125
- weights_down: bfloat16 [16, 2048, 768], P('expert', None, 'tensor'), may hold values from -0.21875 to 0.21875
- cotangent: bfloat16 [256, 2048], P(('dp', 'expert')), may hold values from -6 to 6
Outputs:
- layer_out: bfloat16 [256, 2048], P(('dp', 'expert'), 'tensor')
- tokens_grad: bfloat16 [256, 2048], P(('dp', 'expert'), 'tensor')
- gate_up_grad: bfloat16 [16, 2048, 2, 768], P('expert', 'dp', None, 'tensor')
- down_grad: bfloat16 [16, 2048, 768], P('expert', 'dp', 'tensor')
Inputs may be any that keep to these rules, and one draw needn't show every extreme that they name: `routes`: each row names 8 different experts. Among the 16 rows of one index of dp and expert no expert is named more than 16 times, a bound that some block reaches.
All inputs are finite; a program needn't handle non-finite values.
Results may differ from a plain program's by a relative error of at most 0.0072.
Values may be sent and summed in bfloat16 or wider, within the bound.
A program may use at most 64 MiB of HBM per device.

v0:
```python
import jax
import jax.numpy as jnp
from jax import lax
from jax.sharding import PartitionSpec as P

F32 = jnp.float32
BF16 = jnp.bfloat16


def cut(value):
    return lax.reduce_precision(value, exponent_bits=8, mantissa_bits=7)


def body(tokens, routes, route_weight, weights_gate_up, weights_down, cotangent):
    tok_rows, width = tokens.shape
    expert_local = weights_gate_up.shape[0]
    n_expert = lax.axis_size("expert")
    n_tensor = lax.axis_size("tensor")
    n_dp = lax.axis_size("dp")
    expert_total = expert_local * n_expert
    group = tok_rows * n_expert
    my_dp = lax.axis_index("dp")
    chosen = routes[:, :, None] == jnp.arange(expert_total, dtype=jnp.int32)[None, None, :]
    dense = jnp.sum(jnp.where(chosen, route_weight[:, :, None], 0.0), axis=1)
    first = cut(dense)
    second = cut(dense - first)
    third = dense - first - second
    parts = jnp.concatenate([first, second, third], axis=1).astype(BF16)
    spare = -parts.shape[1] % 128
    parts = jnp.pad(parts, ((0, 0), (0, spare)))
    sent = jnp.concatenate([tokens, cotangent, parts], axis=1)
    held = lax.all_gather(sent, "expert", axis=0, tiled=True)
    tok = held[:, :width]
    cot = held[:, width : 2 * width]
    parts = held[:, 2 * width : 2 * width + 3 * expert_total].astype(F32)
    parts = parts.reshape(group, 3, expert_total)
    weight = parts[:, 0] + parts[:, 1] + parts[:, 2]
    weight = lax.dynamic_slice_in_dim(
        weight, lax.axis_index("expert") * expert_local, expert_local, axis=1
    ).T[:, :, None]
    share = width // n_dp

    def columns(shift):
        start = lax.rem(my_dp + shift, n_dp) * share
        return jnp.concatenate(
            [
                lax.dynamic_slice_in_dim(tok, start, share, axis=1),
                lax.dynamic_slice_in_dim(cot, start, share, axis=1),
            ],
            axis=1,
        )

    def moved(value, shift):
        return lax.ppermute(value, "dp", [(i, (i + shift) % n_dp) for i in range(n_dp)])

    sides = [columns(0)] + [moved(columns(s), s) for s in range(1, n_dp)]
    gate_up = jnp.einsum("td,edgh->etgh", tok, weights_gate_up, preferred_element_type=F32)
    gate_pre = gate_up[:, :, 0, :]
    up_pre = gate_up[:, :, 1, :]
    sig_gate = jax.nn.sigmoid(gate_pre)
    silu_gate = gate_pre * sig_gate
    hidden = (silu_gate * up_pre * weight).astype(BF16)
    hidden_grad = weight * jnp.einsum("td,edh->eth", cot, weights_down, preferred_element_type=F32)
    gate_grad = (hidden_grad * up_pre * sig_gate * (1.0 + gate_pre * (1.0 - sig_gate))).astype(BF16)
    up_grad = (hidden_grad * silu_gate).astype(BF16)
    mine = jnp.stack([gate_grad, up_grad, hidden], axis=0)
    acts = jnp.concatenate([mine] + [moved(mine, s) for s in range(1, n_dp)], axis=2)
    pre_grads = jnp.stack([gate_grad, up_grad], axis=2)
    out_part = jnp.sum(
        jnp.einsum("eth,edh->etd", hidden, weights_down, preferred_element_type=F32), axis=0
    ).astype(BF16)
    in_part = jnp.sum(
        jnp.einsum("etgh,edgh->etd", pre_grads, weights_gate_up, preferred_element_type=F32), axis=0
    ).astype(BF16)
    both = jnp.stack([out_part, in_part]).reshape(
        2, n_expert, tok_rows, n_tensor, width // n_tensor
    )
    both = both.transpose(1, 3, 0, 2, 4).reshape(
        n_expert * n_tensor, 2, tok_rows, width // n_tensor
    )
    back = lax.all_to_all(both, ("expert", "tensor"), split_axis=0, concat_axis=0, tiled=True)
    results = jnp.sum(back.astype(F32), axis=0).astype(BF16)
    rows = jnp.concatenate(sides, axis=0)
    gate_up_grad = jnp.einsum(
        "td,geth->edgh", rows[:, :share], acts[:2], preferred_element_type=F32
    ).astype(BF16)
    down_grad = jnp.einsum(
        "td,eth->edh", rows[:, share:], acts[2], preferred_element_type=F32
    ).astype(BF16)
    return (results[0], results[1], gate_up_grad, down_grad)


def solution(mesh):
    return jax.shard_map(
        body,
        mesh=mesh,
        in_specs=(
            P(("dp", "expert"), None),
            P(("dp", "expert"), None),
            P(("dp", "expert"), None),
            P("expert", None, None, "tensor"),
            P("expert", None, "tensor"),
            P(("dp", "expert"), None),
        ),
        out_specs=(
            P(("dp", "expert"), "tensor"),
            P(("dp", "expert"), "tensor"),
            P("expert", "dp", None, "tensor"),
            P("expert", "dp", "tensor"),
        ),
        check_vma=False,
    )
```

profile of v0, /device:TPU:0, one launch (start us, length us, event | category | flops | bytes accessed | tf_op | source)
XLA Modules:
  0.0 121.2 jit_solution(4500048296995259462)
XLA Ops:
  7.2 0.9 copy.62
  9.1 1.5 %pad_maximum_fusion.4 = bf16[16,4224]{1,0:T(8,128)(2,1)} fusion(bf16[16,128]{1,0:T(8,128)(2,1)S(1)} %fusion.56, bf16[16,2048]{1,0:T(8,128)(2,1)} %param.11, bf16[16,2048]{1,0:T(8,128)(2,1)} %param.6), kind=kLoop, calls=%fused_computation.63 | loop fusion | flops 405504 | bytes 270336 | tf_op jit(solution)/shard_map/concatenate | solution.py:31
  10.7 25.1 %all-gather.2.cloned.1.call-done = bf16[128,4224]{1,0:T(8,128)(2,1)} async-done(((bf16[16,4224]{1,0:T(8,128)(2,1)}), bf16[128,4224]{1,0:T(8,128)(2,1)}) %all-gather.2.cloned.1.call-update) | async-done | bytes 1081360 | tf_op jit(solution)/shard_map/all_gather | solution.py:32
  36.7 4.0 %fusion.12 = f32[2,128,2,384]{3,1,2,0:T(8,128)S(1)} fusion(bf16[2,2048,2,384]{3,2,1,0:T(2,128)(2,1)} %param.9, bf16[128,4224]{1,0:T(8,128)(2,1)} %all-gather.2.cloned.1.call-done), kind=kOutput, calls=%fused_computation.11 | convolution fusion | flops 805306368 | bytes 7602176 | tf_op jit(solution)/shard_map/td,edgh->etgh/dot_general | solution.py:57
  40.7 0.9 copy-done.4
  41.5 2.0 %fusion.7 = bf16[128,2048]{1,0:T(8,128)(2,1)} fusion(bf16[2,2048,384]{2,1,0:T(8,128)(2,1)S(1)} %copy-done, f32[2,128,2,384]{3,1,2,0:T(8,128)S(1)} %fusion.12, f32[2,128]{1,0:T(2,128)S(1)} %fusion.58), kind=kOutput, calls=%fused_computation.7 | convolution fusion | flops 403603456 | bytes 4457472 | tf_op jit(solution)/shard_map/eth,edh->etd/dot_general | solution.py:70
  43.5 2.2 %stack.28 = bf16[1,8,16,2,1024]{4,3,2,1,0:T(2,128)(2,1)} reshape(bf16[128,2048]{1,0:T(8,128)(2,1)} %fusion.7) | data formatting | bytes 1048576 | tf_op jit(solution)/shard_map/stack | solution.py:75
  45.7 2.0 %copy.68 = bf16[1,8,16,2,1024]{4,2,0,3,1:T(8,128)(2,1)} copy(bf16[1,8,16,2,1024]{4,3,2,1,0:T(2,128)(2,1)} %stack.28) | data formatting | bytes 1048576 | tf_op jit(solution)/shard_map/stack | solution.py:75
  47.7 1.9 %fusion.44 = (bf16[2,128,384]{2,1,0:T(8,128)(2,1)S(1)}, bf16[2,128,384]{2,1,0:T(8,128)(2,1)S(1)}) fusion(f32[2,128,2,384]{3,1,2,0:T(8,128)} %copy-done.4, bf16[2,2048,384]{2,1,0:T(8,128)(2,1)S(1)} %copy-done, bf16[128,4224]{1,0:T(8,128)(2,1)} %all-gather.2.cloned.1.call-done, f32[2,128]{1,0:T(2,128)S(1)} %fusion.58), kind=kOutput, calls=%fused_computation.54 | convolution fusion | flops 404029440 | bytes 4850688 | tf_op jit(solution)/shard_map/td,edh->eth/dot_general | solution.py:63
  50.4 5.8 %fusion.8 = bf16[128,2048]{1,0:T(8,128)(2,1)} fusion(bf16[2,2048,2,384]{3,2,1,0:T(2,128)(2,1)} %param.9, bf16[2,128,1,384]{3,1,0,2:T(8,128)(2,1)S(1)} %bitcast.126, bf16[2,128,1,384]{3,1,0,2:T(8,128)(2,1)S(1)} %bitcast.122), kind=kOutput, calls=%fused_computation.8 | convolution fusion | flops 805765120 | bytes 7208960 | tf_op jit(solution)/shard_map/etgh,edgh->etd/dot_general | solution.py:73
  56.2 2.2 %stack.32 = bf16[1,8,16,2,1024]{4,3,2,1,0:T(2,128)(2,1)} reshape(bf16[128,2048]{1,0:T(8,128)(2,1)} %fusion.8) | data formatting | bytes 1048576 | tf_op jit(solution)/shard_map/stack | solution.py:75
  58.4 1.2 copy.69
  59.6 2.1 %pad_maximum_fusion = bf16[2,8,16,2,1024]{4,2,0,3,1:T(8,128)(2,1)} fusion(bf16[1,8,16,2,1024]{4,2,0,3,1:T(8,128)(2,1)S(1)} %copy.69, bf16[1,8,16,2,1024]{4,2,0,3,1:T(8,128)(2,1)} %copy.68), kind=kLoop, calls=%fused_computation.21 | loop fusion | flops 524288 | bytes 2097152 | tf_op jit(solution)/shard_map/stack | solution.py:75
  61.7 4.4 %all-to-all-start = ((bf16[16,2,16,1024]{3,2,1,0:T(8,128)(2,1)}), bf16[16,2,16,1024]{3,2,1,0:T(8,128)(2,1)}, u32[]{:S(2)}, u32[]{:S(2)}) async-start(bf16[16,2,16,1024]{3,2,1,0:T(8,128)(2,1)} %bitcast.121), calls=%async_computation | async-start | bytes 2097152 | tf_op jit(solution)/shard_map/all_to_all | solution.py:81
  66.2 1.3 %fusion.66 = (bf16[128,2048]{1,0:T(8,128)(2,1)S(1)}, bf16[128,2048]{1,0:T(8,128)(2,1)S(1)}) fusion(bf16[128,4224]{1,0:T(8,128)(2,1)} %all-gather.2.cloned.1.call-done), kind=kLoop, calls=%fused_computation.95 | loop fusion | bytes 2097152 | tf_op jit(solution)/shard_map/slice | solution.py:33
  67.7 1.5 %collective-permute-start.1 = (bf16[128,2048]{1,0:T(8,128)(2,1)S(1)}, bf16[128,2048]{1,0:T(8,128)(2,1)S(1)}, u32[]{:S(2)}, u32[]{:S(2)}) collective-permute-start(bf16[128,2048]{1,0:T(8,128)(2,1)S(1)} %pad_maximum_fusion.3), channel_id=1, source_target_pairs={{0,16},{16,0},{1,17},{17,1},{2,18},{18,2},{3,19},{19,3},{4,20},{20... | collective-permute-start | bytes 1572872 | tf_op jit(solution)/shard_map/ppermute | solution.py:54
  70.1 12.4 %collective-permute-done.1 = bf16[128,2048]{1,0:T(8,128)(2,1)S(1)} collective-permute-done((bf16[128,2048]{1,0:T(8,128)(2,1)S(1)}, bf16[128,2048]{1,0:T(8,128)(2,1)S(1)}, u32[]{:S(2)}, u32[]{:S(2)}) %collective-permute-start.1) | collective-permute-done | bytes 524320 | tf_op jit(solution)/shard_map/ppermute | solution.py:54
  82.6 12.0 %collective-permute-done = bf16[3,2,128,384]{3,2,1,0:T(8,128)(2,1)S(1)} collective-permute-done((bf16[3,2,128,384]{3,2,1,0:T(8,128)(2,1)S(1)}, bf16[3,2,128,384]{3,2,1,0:T(8,128)(2,1)S(1)}, u32[]{:S(2)}, u32[]{:S(2)}) %collective-permute-start) | collective-permute-done | bytes 589856 | tf_op jit(solution)/shard_map/ppermute | solution.py:54
  94.6 0.8 copy-done.6
  95.4 1.8 %fusion.11 = bf16[2,1024,384]{1,2,0:T(8,128)(2,1)} fusion(bf16[256,2048]{1,0:T(8,128)(2,1)S(1)} %pad_maximum_fusion.1, bf16[3,2,128,384]{3,2,1,0:T(8,128)(2,1)S(1)} %collective-permute-done, bf16[1,2,128,384]{3,2,1,0:T(8,128)(2,1)S(1)} %fusion.48, bf16[1,2,128,384]{3,2,1,0:T(8,128)(2,1)S(1)} %bitcast.129, bf16[1,2,128,384]{3,2,1,0:T(8,128)(2,1)S(1)} %bitcast.124), kind=kOutput, calls=%fused_computation.10 | convolution fusion | flops 405012480 | bytes 3276800 | tf_op jit(solution)/shard_map/td,eth->edh/dot_general | solution.py:87
  97.1 2.6 %copy.73 = bf16[2,1024,384]{2,1,0:T(8,128)(2,1)} copy(bf16[2,1024,384]{1,2,0:T(8,128)(2,1)} %fusion.11) | data formatting | bytes 3145728
  99.7 3.9 %convert_bitcast_fusion = bf16[2,1024,2,384]{1,3,0,2:T(8,128)(2,1)} fusion(bf16[3,2,128,384]{3,2,1,0:T(8,128)(2,1)} %copy-done.6, bf16[1,2,128,384]{3,2,1,0:T(8,128)(2,1)S(1)} %fusion.48, bf16[1,2,128,384]{3,2,1,0:T(8,128)(2,1)} %bitcast.127, bf16[1,2,128,384]{3,2,1,0:T(8,128)(2,1)S(1)} %bitcast.125, bf16[256,2048]{1,0:T(8,128)(2,1)} %copy-done.1), kind=kOutput, calls=%fused_computation.4 | convolution fusion | flops 811597824 | bytes 4849664 | tf_op jit(solution)/shard_map/td,geth->edgh/dot_general | solution.py:84
  103.6 8.7 %copy.72 = bf16[2,1024,2,384]{3,2,1,0:T(2,128)(2,1)} copy(bf16[2,1024,2,384]{1,3,0,2:T(8,128)(2,1)} %convert_bitcast_fusion) | data formatting | bytes 6291456
  112.3 1.4 %reduce_sum.23 = bf16[2,16,1024]{2,1,0:T(8,128)(2,1)S(1)} reduce(bf16[16,2,16,1024]{3,2,1,0:T(8,128)(2,1)} %all-to-all-done, bf16[]{:T(256)} %constant.23.clone.1), dimensions={0}, to_apply=%region_1.2 | reduce | flops 491520 | bytes 1114114 | tf_op jit(solution)/shard_map/reduce_sum | solution.py:82
  (30 shorter events, 4.3 us)
Async XLA Ops:
  7.2 34.4 %copy-start = (bf16[2,2048,384]{2,1,0:T(8,128)(2,1)S(1)}, bf16[2,2048,384]{2,1,0:T(8,128)(2,1)}, u32[]{:S(2)}) copy-start(bf16[2,2048,384]{2,1,0:T(8,128)(2,1)} %param.10) | copy-start | bytes 9437188
  7.2 28.6 %all-gather.2.cloned.1.call-start = ((), (), s32[]{:S(2)}) async-start(), calls=%async_computation.1 | async-start | bytes 1216512 | tf_op jit(solution)/shard_map/all_gather | solution.py:32
  40.7 0.9 copy-start.4
  49.7 0.7 copy-start.2
  61.7 50.6 %all-to-all-start = ((bf16[16,2,16,1024]{3,2,1,0:T(8,128)(2,1)}), bf16[16,2,16,1024]{3,2,1,0:T(8,128)(2,1)}, u32[]{:S(2)}, u32[]{:S(2)}) async-start(bf16[16,2,16,1024]{3,2,1,0:T(8,128)(2,1)} %bitcast.121), calls=%async_computation | async-start | bytes 2097152 | tf_op jit(solution)/shard_map/all_to_all | solution.py:81
  66.1 3.0 %copy-start.5 = (f32[2,128,2,384]{3,1,2,0:T(8,128)S(1)}, f32[2,128,2,384]{3,1,2,0:T(8,128)}, u32[]{:S(2)}) copy-start(f32[2,128,2,384]{3,1,2,0:T(8,128)} %copy-done.4) | copy-start | bytes 2359300
  67.5 1.8 %copy-start.3 = (bf16[2,128,384]{2,1,0:T(8,128)(2,1)S(1)}, bf16[2,128,384]{2,1,0:T(8,128)(2,1)}, u32[]{:S(2)}) copy-start(bf16[2,128,384]{2,1,0:T(8,128)(2,1)} %copy-done.2) | copy-start | bytes 589828
  67.7 14.8 %collective-permute-start.1 = (bf16[128,2048]{1,0:T(8,128)(2,1)S(1)}, bf16[128,2048]{1,0:T(8,128)(2,1)S(1)}, u32[]{:S(2)}, u32[]{:S(2)}) collective-permute-start(bf16[128,2048]{1,0:T(8,128)(2,1)S(1)} %pad_maximum_fusion.3), channel_id=1, source_target_pairs={{0,16},{16,0},{1,17},{17,1},{2,18},{18,2},{3,19},{19,3},{4,20},{20... | collective-permute-start | bytes 1572872 | tf_op jit(solution)/shard_map/ppermute | solution.py:54
  69.4 25.1 %collective-permute-start = (bf16[3,2,128,384]{3,2,1,0:T(8,128)(2,1)S(1)}, bf16[3,2,128,384]{3,2,1,0:T(8,128)(2,1)S(1)}, u32[]{:S(2)}, u32[]{:S(2)}) collective-permute-start(bf16[3,2,128,384]{3,2,1,0:T(8,128)(2,1)S(1)} %pad_maximum_fusion.2), channel_id=1, source_target_pairs={{0,16},{16,0},{1,17},{17,1},{2,18},{18,2},{3,19},{19,3},{4,20},{20... | collective-permute-start | bytes 1769480 | tf_op jit(solution)/shard_map/ppermute | solution.py:54
  82.6 12.0 %copy-start.1 = (bf16[256,2048]{1,0:T(8,128)(2,1)}, bf16[256,2048]{1,0:T(8,128)(2,1)S(1)}, u32[]{:S(2)}) copy-start(bf16[256,2048]{1,0:T(8,128)(2,1)S(1)} %pad_maximum_fusion.1) | copy-start | bytes 3145732
  94.6 0.8 copy-start.6
Sparse Core Ops, SparseCore 0:
  10.8 24.9 all-gather.1
where the time goes:
time: 122 us; the launch traced here: 121 us
  waiting for transfers between devices  49.5 us (41%)
  local copies, waits for them, and re-layouts  25.9 us (21%)
  matrix products  19.3 us (16%)
  between operations  14.2 us (12%)
  starting transfers between devices  6.63 us (5%)
  other arithmetic  5.65 us (5%)
    all_gather x1, waiting for transfers between devices, body(): held = lax.all_gather(sent, 'expert', axis=0, tiled=True)  25.1 us
    ppermute x2, waiting for transfers between devices, moved(): lax.ppermute(value, 'dp', [(i, (i + shift) % n_dp) for i in range(n_dp)])  24.4 us
    unnamed x19, local copies, waits for them, and re-layouts  15.4 us
    another operation x4, local copies, waits for them, and re-layouts, body(): jnp.stack([out_part, in_part])  7.64 us
    dot_general x1, matrix products, body(): jnp.einsum('etgh,edgh->etd', pre_grads, weights_gate_up, preferred_elemen...  5.78 us
    all_to_all x1, starting transfers between devices, body(): lax.all_to_all(both, ('expert', 'tensor'), split_axis=0, concat_axis=0, t...  4.42 us
    dot_general x1, matrix products, body(): jnp.einsum('td,edgh->etgh', tok, weights_gate_up, preferred_element_type=...  3.95 us
    dot_general x1, matrix products, body(): jnp.einsum('td,geth->edgh', rows[:, :share], acts[:2], preferred_element_...  3.9 us
  transfers between devices with their start and end apart: 4, of which 3 were waited for; matrix products, arithmetic and copies ran while one was open for 15% of the time, Pallas kernels for 0%

commit v1 on v0

--- a/solution.py
+++ b/solution.py
@@ -1,10 +1,39 @@
+import functools
 import jax
 import jax.numpy as jnp
 from jax import lax
 from jax.sharding import PartitionSpec as P
+from jax.lax import axis_index, axis_size, ppermute
 
 F32 = jnp.float32
 BF16 = jnp.bfloat16
+
+
+def mix_the_desk(array_in, ndim_at):
+    array_in = jnp.moveaxis(array_in, 0, ndim_at)
+    lower = array_in.shape
+    return array_in.reshape(
+        *lower[:ndim_at], lower[ndim_at] * lower[ndim_at + 1], *lower[ndim_at + 2 :]
+    )
+
+
+def enter_ports(block_in, axis_id):
+    v_now = block_in[None]
+    amount_of = axis_size(axis_id)
+    for i0 in range(amount_of.bit_length() - 1):
+        local_part = 1 << i0
+        finding = ppermute(v_now, axis_id, [(w, w ^ local_part) for w in range(amount_of)])
+        known = jnp.stack([v_now, finding], 0)
+        oldest = axis_index(axis_id) >> i0 & 1
+        v_now = jnp.where(oldest == 0, known, known[::-1]).reshape(-1, *block_in.shape)
+    return v_now
+
+
+def sections_compute(u, local_array, array_dim):
+    return mix_the_desk(enter_ports(u, local_array), array_dim)
+
+
+switch_forms_up = functools.partial(sections_compute, local_array="expert", array_dim=0)
 
 
 def cut(value):
@@ -29,7 +58,7 @@
     spare = -parts.shape[1] % 128
     parts = jnp.pad(parts, ((0, 0), (0, spare)))
     sent = jnp.concatenate([tokens, cotangent, parts], axis=1)
-    held = lax.all_gather(sent, "expert", axis=0, tiled=True)
+    held = switch_forms_up(sent)
     tok = held[:, :width]
     cot = held[:, width : 2 * width]
     parts = held[:, 2 * width : 2 * width + 3 * expert_total].astype(F32)

time: 122 us -> 125 us (1.025)
  between operations: 14.2 us -> 0.84 us
  starting transfers between devices: 6.63 us -> 14.1 us
  waiting for transfers between devices: 49.5 us -> 56.3 us
  other arithmetic: 5.65 us -> 9.22 us
  local copies, waits for them, and re-layouts: 25.9 us -> 24.5 us
    ppermute x0 -> x3, waiting for transfers between devices: none -> 32 us  [enter_ports(): ppermute(v_now, axis_id, [(w, w ^ local_part) for w in range(amount_of)])]
    all_gather x1 -> x0, waiting for transfers between devices: 25.1 us -> none  [body(): held = lax.all_gather(sent, 'expert', axis=0, tiled=True)]
    ppermute x0 -> x3, starting transfers between devices: none -> 6.21 us  [enter_ports(): ppermute(v_now, axis_id, [(w, w ^ local_part) for w in range(amount_of)])]
    another operation x1 -> x6, other arithmetic: 0.01 us -> 4.02 us  [the longest x5 4.02 us: enter_ports(): known = jnp.stack([v_now, finding], 0)]
    concatenate x1 -> x0, other arithmetic: 1.54 us -> none  [body(): sent = jnp.concatenate([tokens, cotangent, parts], axis=1)]
    all_to_all x1, starting transfers between devices: 4.42 us -> 5.73 us  [body(): lax.all_to_all(both, ('expert', 'tensor'), split_axis=0, concat_axis=0, t...]
    unnamed x19 -> x21, local copies, waits for them, and re-layouts: 15.4 us -> 14.9 us
  transfers between devices with their start and end apart: 4 -> 6, of which waited for: 3 -> 5; matrix products, arithmetic and copies ran while one was open for 15% -> 15% of each run, Pallas kernels for 0% -> 0%
where the time goes in v1:
time: 125 us; the launch traced here: 124 us
  waiting for transfers between devices  56.3 us (45%)
  local copies, waits for them, and re-layouts  24.5 us (20%)
  matrix products  19.4 us (16%)
  starting transfers between devices  14.1 us (11%)
  other arithmetic  9.22 us (7%)
    ppermute x3, waiting for transfers between devices, enter_ports(): ppermute(v_now, axis_id, [(w, w ^ local_part) for w in range(amount_of)])  32 us
    ppermute x2, waiting for transfers between devices, moved(): lax.ppermute(value, 'dp', [(i, (i + shift) % n_dp) for i in range(n_dp)])  24.3 us
    unnamed x21, local copies, waits for them, and re-layouts  14.9 us
    another operation x4, local copies, waits for them, and re-layouts, body(): jnp.stack([out_part, in_part])  7.58 us
    ppermute x3, starting transfers between devices, enter_ports(): ppermute(v_now, axis_id, [(w, w ^ local_part) for w in range(amount_of)])  6.21 us
    dot_general x1, matrix products, body(): jnp.einsum('etgh,edgh->etd', pre_grads, weights_gate_up, preferred_elemen...  5.8 us
    all_to_all x1, starting transfers between devices, body(): lax.all_to_all(both, ('expert', 'tensor'), split_axis=0, concat_axis=0, t...  5.73 us
    another operation x5, other arithmetic, enter_ports(): known = jnp.stack([v_now, finding], 0)  4.02 us
  transfers between devices with their start and end apart: 6, of which 5 were waited for; matrix products, arithmetic and copies ran while one was open for 15% of the time, Pallas kernels for 0%

profile of v1, /device:TPU:0, one launch (start us, length us, event | category | flops | bytes accessed | tf_op | source)
XLA Modules:
  0.0 124.4 jit_solution(9240159644654613246)
XLA Ops:
  5.8 2.9 %collective-permute-start.1 = (bf16[2,16,4224]{2,1,0:T(8,128)(2,1)}, bf16[2,16,4224]{2,1,0:T(8,128)(2,1)}, u32[]{:S(2)}, u32[]{:S(2)}) collective-permute-start(bf16[2,16,4224]{2,1,0:T(8,128)(2,1)} %get-tuple-element.33), channel_id=1, source_target_pairs={{0,4},{2,6},{4,0},{6,2},{8,12},{10,14},{12,8},{14,10},{1,5},{3,7},... | collective-permute-start | bytes 811016 | tf_op jit(solution)/shard_map/ppermute | solution.py:25
  8.7 7.1 %collective-permute-done.1 = bf16[2,16,4224]{2,1,0:T(8,128)(2,1)} collective-permute-done((bf16[2,16,4224]{2,1,0:T(8,128)(2,1)}, bf16[2,16,4224]{2,1,0:T(8,128)(2,1)}, u32[]{:S(2)}, u32[]{:S(2)}) %collective-permute-start.1) | collective-permute-done | bytes 270368 | tf_op jit(solution)/shard_map/ppermute | solution.py:25
  17.7 2.8 %collective-permute-start.2 = (bf16[4,16,4224]{2,1,0:T(8,128)(2,1)}, bf16[4,16,4224]{2,1,0:T(8,128)(2,1)}, u32[]{:S(2)}, u32[]{:S(2)}) collective-permute-start(bf16[4,16,4224]{2,1,0:T(8,128)(2,1)} %bitcast.7), channel_id=1, source_target_pairs={{0,8},{2,10},{4,12},{6,14},{8,0},{10,2},{12,4},{14,6},{1,9},{3,11}... | collective-permute-start | bytes 1622024 | tf_op jit(solution)/shard_map/ppermute | solution.py:25
  20.5 23.9 %collective-permute-done.2 = bf16[4,16,4224]{2,1,0:T(8,128)(2,1)} collective-permute-done((bf16[4,16,4224]{2,1,0:T(8,128)(2,1)}, bf16[4,16,4224]{2,1,0:T(8,128)(2,1)}, u32[]{:S(2)}, u32[]{:S(2)}) %collective-permute-start.2) | collective-permute-done | bytes 540704 | tf_op jit(solution)/shard_map/ppermute | solution.py:25
  44.3 1.3 %pad_maximum_fusion = bf16[2,4,16,4224]{3,2,1,0:T(8,128)(2,1)S(1)} fusion(bf16[1,4,16,4224]{3,2,1,0:T(8,128)(2,1)} %bitcast.8, bf16[1,4,16,4224]{3,2,1,0:T(8,128)(2,1)} %bitcast.6), kind=kLoop, calls=%fused_computation.22 | loop fusion | flops 540672 | bytes 2162688 | tf_op jit(solution)/shard_map/stack | solution.py:26
  46.9 4.0 %fusion.12 = f32[2,128,2,384]{3,1,2,0:T(8,128)S(1)} fusion(bf16[2,2048,2,384]{3,2,1,0:T(2,128)(2,1)} %param.9, bf16[128,4224]{1,0:T(8,128)(2,1)} %bitcast.136), kind=kOutput, calls=%fused_computation.12 | convolution fusion | flops 805306368 | bytes 7602176 | tf_op jit(solution)/shard_map/td,edgh->etgh/dot_general | solution.py:86
  50.9 2.0 %fusion.44 = (bf16[2,128,384]{2,1,0:T(8,128)(2,1)S(1)}, bf16[2,128,384]{2,1,0:T(8,128)(2,1)S(1)}) fusion(f32[2,128,2,384]{3,1,2,0:T(8,128)S(1)} %fusion.12, bf16[2,2048,384]{2,1,0:T(8,128)(2,1)S(1)} %copy-done, bf16[128,4224]{1,0:T(8,128)(2,1)} %bitcast.137, f32[2,128]{1,0:T(2,128)S(1)} %fusion.62), kind=kOutput, calls=%fused_computation.59 | convolution fusion | flops 404029440 | bytes 4850688 | tf_op jit(solution)/shard_map/td,edh->eth/dot_general | solution.py:92
  52.9 1.9 %fusion.7 = bf16[128,2048]{1,0:T(8,128)(2,1)} fusion(bf16[2,2048,384]{2,1,0:T(8,128)(2,1)S(1)} %copy-done, f32[2,128,2,384]{3,1,2,0:T(8,128)S(1)} %fusion.12, f32[2,128]{1,0:T(2,128)S(1)} %fusion.62), kind=kOutput, calls=%fused_computation.7 | convolution fusion | flops 403603456 | bytes 4457472 | tf_op jit(solution)/shard_map/eth,edh->etd/dot_general | solution.py:99
  54.9 2.2 %stack.52 = bf16[1,8,16,2,1024]{4,3,2,1,0:T(2,128)(2,1)} reshape(bf16[128,2048]{1,0:T(8,128)(2,1)} %fusion.7) | data formatting | bytes 1048576 | tf_op jit(solution)/shard_map/stack | solution.py:104
  57.1 2.0 %copy.66 = bf16[1,8,16,2,1024]{4,2,0,3,1:T(8,128)(2,1)} copy(bf16[1,8,16,2,1024]{4,3,2,1,0:T(2,128)(2,1)} %stack.52) | data formatting | bytes 1048576 | tf_op jit(solution)/shard_map/stack | solution.py:104
  59.1 5.8 %fusion.8 = bf16[128,2048]{1,0:T(8,128)(2,1)} fusion(bf16[2,2048,2,384]{3,2,1,0:T(2,128)(2,1)} %param.9, bf16[2,128,1,384]{3,1,0,2:T(8,128)(2,1)S(1)} %bitcast.144, bf16[2,128,1,384]{3,1,0,2:T(8,128)(2,1)S(1)} %bitcast.140), kind=kOutput, calls=%fused_computation.8 | convolution fusion | flops 805765120 | bytes 7208960 | tf_op jit(solution)/shard_map/etgh,edgh->etd/dot_general | solution.py:102
  64.9 2.2 %stack.56 = bf16[1,8,16,2,1024]{4,3,2,1,0:T(2,128)(2,1)} reshape(bf16[128,2048]{1,0:T(8,128)(2,1)} %fusion.8) | data formatting | bytes 1048576 | tf_op jit(solution)/shard_map/stack | solution.py:104
  67.1 1.2 copy.67
  68.3 2.2 %pad_maximum_fusion.1 = bf16[2,8,16,2,1024]{4,2,0,3,1:T(8,128)(2,1)} fusion(bf16[1,8,16,2,1024]{4,2,0,3,1:T(8,128)(2,1)S(1)} %copy.67, bf16[1,8,16,2,1024]{4,2,0,3,1:T(8,128)(2,1)} %copy.66), kind=kLoop, calls=%fused_computation.23 | loop fusion | flops 524288 | bytes 2097152 | tf_op jit(solution)/shard_map/stack | solution.py:104
  70.4 5.7 %all-to-all-start = ((bf16[16,2,16,1024]{3,2,1,0:T(8,128)(2,1)}), bf16[16,2,16,1024]{3,2,1,0:T(8,128)(2,1)}, u32[]{:S(2)}, u32[]{:S(2)}) async-start(bf16[16,2,16,1024]{3,2,1,0:T(8,128)(2,1)} %bitcast.139), calls=%async_computation | async-start | bytes 2097152 | tf_op jit(solution)/shard_map/all_to_all | solution.py:110
  76.2 1.3 %fusion.70 = (bf16[128,2048]{1,0:T(8,128)(2,1)S(1)}, bf16[128,2048]{1,0:T(8,128)(2,1)S(1)}) fusion(bf16[128,4224]{1,0:T(8,128)(2,1)} %bitcast.138), kind=kLoop, calls=%fused_computation.105 | loop fusion | bytes 2097152 | tf_op jit(solution)/shard_map/slice | solution.py:62
  77.7 1.6 %collective-permute-start.4 = (bf16[128,2048]{1,0:T(8,128)(2,1)S(1)}, bf16[128,2048]{1,0:T(8,128)(2,1)S(1)}, u32[]{:S(2)}, u32[]{:S(2)}) collective-permute-start(bf16[128,2048]{1,0:T(8,128)(2,1)S(1)} %pad_maximum_fusion.5), channel_id=1, source_target_pairs={{0,16},{16,0},{1,17},{17,1},{2,18},{18,2},{3,19},{19,3},{4,20},{20... | collective-permute-start | bytes 1572872 | tf_op jit(solution)/shard_map/ppermute | solution.py:83
  80.1 12.4 %collective-permute-done.4 = bf16[128,2048]{1,0:T(8,128)(2,1)S(1)} collective-permute-done((bf16[128,2048]{1,0:T(8,128)(2,1)S(1)}, bf16[128,2048]{1,0:T(8,128)(2,1)S(1)}, u32[]{:S(2)}, u32[]{:S(2)}) %collective-permute-start.4) | collective-permute-done | bytes 524320 | tf_op jit(solution)/shard_map/ppermute | solution.py:83
  92.6 12.0 %collective-permute-done.3 = bf16[3,2,128,384]{3,2,1,0:T(8,128)(2,1)S(1)} collective-permute-done((bf16[3,2,128,384]{3,2,1,0:T(8,128)(2,1)S(1)}, bf16[3,2,128,384]{3,2,1,0:T(8,128)(2,1)S(1)}, u32[]{:S(2)}, u32[]{:S(2)}) %collective-permute-start.3) | collective-permute-done | bytes 589856 | tf_op jit(solution)/shard_map/ppermute | solution.py:83
  105.4 1.8 %fusion.11 = bf16[2,1024,384]{1,2,0:T(8,128)(2,1)} fusion(bf16[256,2048]{1,0:T(8,128)(2,1)S(1)} %pad_maximum_fusion.2, bf16[3,2,128,384]{3,2,1,0:T(8,128)(2,1)S(1)} %collective-permute-done.3, bf16[1,2,128,384]{3,2,1,0:T(8,128)(2,1)S(1)} %fusion.48, bf16[1,2,128,384]{3,2,1,0:T(8,128)(2,1)S(1)} %bitcast.147, bf16[1,2,128,384]{3,2,1,0:T(8,128)(2,1)S(1)} %bitcast.142), kind=kOutput, calls=%fused_computation.11 | convolution fusion | flops 405012480 | bytes 3276800 | tf_op jit(solution)/shard_map/td,eth->edh/dot_general | solution.py:116
  107.2 2.6 %copy.71 = bf16[2,1024,384]{2,1,0:T(8,128)(2,1)} copy(bf16[2,1024,384]{1,2,0:T(8,128)(2,1)} %fusion.11) | data formatting | bytes 3145728
  109.7 3.9 %convert_bitcast_fusion = bf16[2,1024,2,384]{1,3,0,2:T(8,128)(2,1)} fusion(bf16[3,2,128,384]{3,2,1,0:T(8,128)(2,1)} %copy-done.7, bf16[1,2,128,384]{3,2,1,0:T(8,128)(2,1)S(1)} %fusion.48, bf16[1,2,128,384]{3,2,1,0:T(8,128)(2,1)} %bitcast.145, bf16[1,2,128,384]{3,2,1,0:T(8,128)(2,1)S(1)} %bitcast.143, bf16[256,2048]{1,0:T(8,128)(2,1)} %copy-done.2), kind=kOutput, calls=%fused_computation.4 | convolution fusion | flops 811597824 | bytes 4849664 | tf_op jit(solution)/shard_map/td,geth->edgh/dot_general | solution.py:113
  113.7 8.7 %copy.70 = bf16[2,1024,2,384]{3,2,1,0:T(2,128)(2,1)} copy(bf16[2,1024,2,384]{1,3,0,2:T(8,128)(2,1)} %convert_bitcast_fusion) | data formatting | bytes 6291456
  122.3 1.4 %reduce_sum.23 = bf16[2,16,1024]{2,1,0:T(8,128)(2,1)S(1)} reduce(bf16[16,2,16,1024]{3,2,1,0:T(8,128)(2,1)} %all-to-all-done, bf16[]{:T(256)} %constant.28.clone.1), dimensions={0}, to_apply=%region_1.2 | reduce | flops 491520 | bytes 1114114 | tf_op jit(solution)/shard_map/reduce_sum | solution.py:111
  (41 shorter events, 10.8 us)
Async XLA Ops:
  0.6 50.3 %copy-start = (bf16[2,2048,384]{2,1,0:T(8,128)(2,1)S(1)}, bf16[2,2048,384]{2,1,0:T(8,128)(2,1)}, u32[]{:S(2)}) copy-start(bf16[2,2048,384]{2,1,0:T(8,128)(2,1)} %param.10) | copy-start | bytes 9437188
  3.5 1.5 %collective-permute-start = (bf16[1,16,4224]{2,1,0:T(8,128)(2,1)S(1)}, bf16[1,16,4224]{2,1,0:T(8,128)(2,1)S(1)}, u32[]{:S(2)}, u32[]{:S(2)}) collective-permute-start(bf16[1,16,4224]{2,1,0:T(8,128)(2,1)S(1)} %get-tuple-element.35), channel_id=1, source_target_pairs={{0,2},{2,0},{4,6},{6,4},{8,10},{10,8},{12,14},{14,12},{1,3},{3,1},... | collective-permute-start | bytes 405512 | tf_op jit(solution)/shard_map/ppermute | solution.py:25
  5.8 10.0 %collective-permute-start.1 = (bf16[2,16,4224]{2,1,0:T(8,128)(2,1)}, bf16[2,16,4224]{2,1,0:T(8,128)(2,1)}, u32[]{:S(2)}, u32[]{:S(2)}) collective-permute-start(bf16[2,16,4224]{2,1,0:T(8,128)(2,1)} %get-tuple-element.33), channel_id=1, source_target_pairs={{0,4},{2,6},{4,0},{6,2},{8,12},{10,14},{12,8},{14,10},{1,5},{3,7},... | collective-permute-start | bytes 811016 | tf_op jit(solution)/shard_map/ppermute | solution.py:25
  17.7 26.6 %collective-permute-start.2 = (bf16[4,16,4224]{2,1,0:T(8,128)(2,1)}, bf16[4,16,4224]{2,1,0:T(8,128)(2,1)}, u32[]{:S(2)}, u32[]{:S(2)}) collective-permute-start(bf16[4,16,4224]{2,1,0:T(8,128)(2,1)} %bitcast.7), channel_id=1, source_target_pairs={{0,8},{2,10},{4,12},{6,14},{8,0},{10,2},{12,4},{14,6},{1,9},{3,11}... | collective-permute-start | bytes 1622024 | tf_op jit(solution)/shard_map/ppermute | solution.py:25
  45.8 1.0 copy-start.1
  50.9 2.0 %copy-start.5 = (f32[2,128,2,384]{3,1,2,0:T(8,128)}, f32[2,128,2,384]{3,1,2,0:T(8,128)S(1)}, u32[]{:S(2)}) copy-start(f32[2,128,2,384]{3,1,2,0:T(8,128)S(1)} %fusion.12) | copy-start | bytes 2359300
  52.9 6.1 %copy-start.3 = (bf16[2,128,384]{2,1,0:T(8,128)(2,1)}, bf16[2,128,384]{2,1,0:T(8,128)(2,1)S(1)}, u32[]{:S(2)}) copy-start(bf16[2,128,384]{2,1,0:T(8,128)(2,1)S(1)} %get-tuple-element.25) | copy-start | bytes 589828
  70.4 51.9 %all-to-all-start = ((bf16[16,2,16,1024]{3,2,1,0:T(8,128)(2,1)}), bf16[16,2,16,1024]{3,2,1,0:T(8,128)(2,1)}, u32[]{:S(2)}, u32[]{:S(2)}) async-start(bf16[16,2,16,1024]{3,2,1,0:T(8,128)(2,1)} %bitcast.139), calls=%async_computation | async-start | bytes 2097152 | tf_op jit(solution)/shard_map/all_to_all | solution.py:110
  76.2 3.1 %copy-start.6 = (f32[2,128,2,384]{3,1,2,0:T(8,128)S(1)}, f32[2,128,2,384]{3,1,2,0:T(8,128)}, u32[]{:S(2)}) copy-start(f32[2,128,2,384]{3,1,2,0:T(8,128)} %copy-done.5) | copy-start | bytes 2359300
  77.5 1.9 %copy-start.4 = (bf16[2,128,384]{2,1,0:T(8,128)(2,1)S(1)}, bf16[2,128,384]{2,1,0:T(8,128)(2,1)}, u32[]{:S(2)}) copy-start(bf16[2,128,384]{2,1,0:T(8,128)(2,1)} %copy-done.3) | copy-start | bytes 589828
  77.7 14.8 %collective-permute-start.4 = (bf16[128,2048]{1,0:T(8,128)(2,1)S(1)}, bf16[128,2048]{1,0:T(8,128)(2,1)S(1)}, u32[]{:S(2)}, u32[]{:S(2)}) collective-permute-start(bf16[128,2048]{1,0:T(8,128)(2,1)S(1)} %pad_maximum_fusion.5), channel_id=1, source_target_pairs={{0,16},{16,0},{1,17},{17,1},{2,18},{18,2},{3,19},{19,3},{4,20},{20... | collective-permute-start | bytes 1572872 | tf_op jit(solution)/shard_map/ppermute | solution.py:83
  79.5 25.1 %collective-permute-start.3 = (bf16[3,2,128,384]{3,2,1,0:T(8,128)(2,1)S(1)}, bf16[3,2,128,384]{3,2,1,0:T(8,128)(2,1)S(1)}, u32[]{:S(2)}, u32[]{:S(2)}) collective-permute-start(bf16[3,2,128,384]{3,2,1,0:T(8,128)(2,1)S(1)} %pad_maximum_fusion.3), channel_id=1, source_target_pairs={{0,16},{16,0},{1,17},{17,1},{2,18},{18,2},{3,19},{19,3},{4,20},{20... | collective-permute-start | bytes 1769480 | tf_op jit(solution)/shard_map/ppermute | solution.py:83
  92.6 12.0 %copy-start.2 = (bf16[256,2048]{1,0:T(8,128)(2,1)}, bf16[256,2048]{1,0:T(8,128)(2,1)S(1)}, u32[]{:S(2)}) copy-start(bf16[256,2048]{1,0:T(8,128)(2,1)S(1)} %pad_maximum_fusion.2) | copy-start | bytes 3145732
  104.6 0.8 copy-start.7
